TPU v7x, 32 devices: a whole 2x2x4 slice. The times are simulated.
32 devices in a mesh: tp: 2 (over x), seq: 16 (over z, y, core).
Axes of the slice: x: 2, y: 2, z: 4, core: 2. Of those that a mesh axis runs over, the one named last changes fastest.
Arguments:
- llama_context: bfloat16 [128, 4096], P(None, 'tp'), may hold values from -6 to 6
- llama_residual: bfloat16 [128, 4096], P(None, 'seq'), may hold values from -6 to 6
- w_attn_out: bfloat16 [4096, 4096], P('tp', 'seq'), may hold values from -0.09375 to 0.09375
- w_caption: bfloat16 [4096, 2560], P('seq', 'tp'), may hold values from -0.09375 to 0.09375
- w_text_kv: bfloat16 [2560, 2, 2048], P(None, None, 'tp'), may hold values from -0.125 to 0.125
- prompt_length: int32 [1], replicated, may hold values from 1 to 128, as said below
- image_query: bfloat16 [2, 4096, 2048], P(None, 'seq', 'tp'), may hold values from -32 to 32
- image_key: bfloat16 [2, 4096, 2048], P(None, 'seq', 'tp'), may hold values from -9 to 9
- image_value: bfloat16 [2, 4096, 2048], P(None, 'seq', 'tp'), may hold values from -6 to 6
Outputs:
- joint_context: bfloat16 [2, 4096, 2048], P(None, 'seq', 'tp')
Inputs may be any that keep to these rules, and one draw needn't show every extreme that they name: `prompt_length`: one pair's prompt has all 128 tokens live, every other pair's fewer.
All inputs are finite; a program needn't handle non-finite values.
Results may differ from a plain program's by a relative error of at most 0.039.
Values may be sent and summed in bfloat16 or wider, within the bound.
A program may use at most 192 MiB of HBM per device.

v0:
```python
import functools
import math

import jax
import jax.numpy as jnp
from jax import lax
from jax.experimental import pallas as pl
from jax.experimental.pallas import tpu as pltpu
from jax.sharding import PartitionSpec as P

TXT = 128
HD = 128
IMG = 4096
CHUNK = 1024
FACTOR = math.log2(math.e) / math.sqrt(HD)
NT = (((1,), (1,)), ((), ()))


def flip(index, step, count):
    result = 0
    bit = 1
    while bit < count:
        result = result + ((index // bit + step // bit) % 2) * bit
        bit *= 2
    return result


def mixed_step(place, count):
    odd = place % 2
    return (1 - odd) * (count // 2 + place // 2) + odd * ((place + 1) // 2)


def attend_kernel(
    group,
    sides,
    heads,
    seq_count,
    tp_count,
    query,
    key,
    value,
    context,
    residual,
    w_out,
    w_caption,
    w_head,
    bias,
    out,
    key_land,
    value_land,
    query_land,
    terms,
    parts,
    parts_land,
    states,
    text_key,
    text_value,
    result,
    own_sem,
    send_sem,
    recv_sem,
    term_send,
    term_recv,
    part_send,
    part_recv,
    state_send,
    state_recv,
    side_send,
    side_recv,
):
    units = sides * heads
    rows = query.shape[1]
    query_rows = query_land.shape[1]
    seq_index = lax.axis_index("seq")
    tp_index = lax.axis_index("tp")
    base = seq_index // group * group
    member = seq_index % group

    def unit_of(who):
        unit = who % units
        return unit // heads, unit % heads, who // units

    def columns(head):
        return pl.ds(pl.multiple_of(head * HD, HD), HD)

    barrier = pltpu.get_barrier_semaphore()

    @pl.loop(1, seq_count)
    def _(step):
        pl.semaphore_signal(
            barrier,
            inc=1,
            device_id={"seq": flip(seq_index, step, seq_count)},
            device_id_type=pl.DeviceIdType.MESH,
        )

    for step in range(1, tp_count):
        pl.semaphore_signal(
            barrier,
            inc=1,
            device_id={"tp": flip(tp_index, step, tp_count)},
            device_id_type=pl.DeviceIdType.MESH,
        )
    pl.semaphore_wait(barrier, seq_count + tp_count - 2)

    def transfer(axis, who, source, target, sent, landed):
        return pltpu.make_async_remote_copy(
            src_ref=source,
            dst_ref=target,
            send_sem=sent,
            recv_sem=landed,
            device_id={axis: who},
            device_id_type=pl.DeviceIdType.MESH,
        )

    def remote(kind, who, source, target):
        return pltpu.make_async_remote_copy(
            src_ref=source,
            dst_ref=target,
            send_sem=send_sem.at[kind, who],
            recv_sem=recv_sem.at[kind, member],
            device_id={"seq": base + who},
            device_id_type=pl.DeviceIdType.MESH,
        )

    def arrival(kind, who, target):
        return pltpu.make_async_remote_copy(
            src_ref=target,
            dst_ref=target,
            send_sem=send_sem.at[kind, who],
            recv_sem=recv_sem.at[kind, who],
            device_id={"seq": base + who},
            device_id_type=pl.DeviceIdType.MESH,
        )

    def sources(who):
        side, head, part = unit_of(who)
        cols = columns(head)
        first = pl.multiple_of(part * query_rows, query_rows)
        return (
            key.at[side, :, cols],
            value.at[side, :, cols],
            query.at[side, pl.ds(first, query_rows), cols],
        )

    def landings(who):
        return (
            key_land.at[who, :, pl.ds(0, HD)],
            value_land.at[who, :, pl.ds(0, HD)],
            query_land.at[who],
        )

    def out_place(who):
        side, head, part = unit_of(who)
        first = pl.multiple_of(part * query_rows, query_rows)
        return out.at[side, pl.ds(first, query_rows), columns(head)]

    mine_from = sources(member)
    mine_to = landings(member)
    own = [
        pltpu.make_async_copy(mine_from[kind], mine_to[kind], own_sem.at[kind]) for kind in range(3)
    ]
    def send(kind, step):
        who = flip(member, step, group)
        remote(kind, who, sources(who)[kind], landings(member)[kind]).start()

    def wave(kind, first, last):
        @pl.loop(first, last)
        def _(place):
            send(kind, mixed_step(place, group))

    half = group // 2
    wave(0, 0, half)
    for copy in own:
        copy.start()

    term = jnp.dot(context[...], w_out[...], preferred_element_type=jnp.float32)
    terms[tp_index] = term.astype(jnp.bfloat16)
    for step in range(1, tp_count):
        other = flip(tp_index, step, tp_count)
        mine = terms.at[tp_index]
        transfer("tp", other, mine, mine, term_send.at[other], term_recv.at[tp_index]).start()
    wave(0, half, group - 1)
    value_land[:, :, HD:] = jnp.ones((group, rows, HD), jnp.bfloat16)
    text_value[:, HD:] = jnp.ones((TXT, HD), jnp.bfloat16)
    for step in range(1, tp_count):
        other = flip(tp_index, step, tp_count)
        theirs = terms.at[other]
        transfer("tp", other, theirs, theirs, term_send.at[other], term_recv.at[other]).wait_recv()
    attended = terms[0].astype(jnp.float32)
    for index in range(1, tp_count):
        attended = attended + terms[index].astype(jnp.float32)
    hidden = (residual[...].astype(jnp.float32) + attended).astype(jnp.bfloat16)
    caption = jnp.dot(hidden, w_caption[...], preferred_element_type=jnp.float32)
    parts[...] = caption.reshape(parts.shape).astype(jnp.bfloat16)

    def part_copy(who, landed):
        return transfer(
            "seq",
            who,
            parts.at[who],
            parts_land.at[landed],
            part_send.at[who],
            part_recv.at[landed],
        )

    @pl.loop(1, seq_count)
    def _(step):
        part_copy(flip(seq_index, seq_count - step, seq_count), seq_index).start()

    parts_land[seq_index] = parts[seq_index]
    wave(1, 0, half)

    @pl.loop(1, seq_count)
    def _(step):
        who = flip(seq_index, seq_count - step, seq_count)
        part_copy(who, who).wait_recv()

    summed = jnp.sum(parts_land[...].astype(jnp.float32), axis=0)
    states[tp_index, member] = summed.astype(jnp.bfloat16)

    def state_copy(who, owner):
        place = states.at[tp_index, owner]
        return transfer(
            "seq", base + who, place, place, state_send.at[who], state_recv.at[owner]
        )

    @pl.loop(1, group)
    def _(step):
        state_copy(flip(member, group - step, group), member).start()

    wave(1, half, group - 1)

    @pl.loop(1, group)
    def _(step):
        who = flip(member, group - step, group)
        state_copy(who, who).wait_recv()

    for step in range(1, tp_count):
        other = flip(tp_index, step, tp_count)
        mine = states.at[tp_index]
        transfer("tp", other, mine, mine, side_send.at[other], side_recv.at[tp_index]).start()

    @pl.loop(0, group - 1)
    def _(place):
        send(2, group - 1 - place)

    for step in range(1, tp_count):
        other = flip(tp_index, step, tp_count)
        theirs = states.at[other]
        transfer("tp", other, theirs, theirs, side_send.at[other], side_recv.at[other]).wait_recv()
    depth = w_caption.shape[1]
    text = jnp.zeros((TXT, 2 * HD), jnp.float32)
    for index in range(tp_count):
        block = states[index].astype(jnp.float32).reshape(TXT, depth).astype(jnp.bfloat16)
        text = text + jnp.dot(
            block,
            w_head[index * depth : (index + 1) * depth],
            preferred_element_type=jnp.float32,
        )
    text = text.astype(jnp.bfloat16)
    text_key[:, :HD] = text[:, :HD]
    text_key[:, HD:] = text[:, :HD]
    text_value[:, :HD] = text[:, HD:]

    for copy in own:
        copy.wait()

    @pl.loop(0, group - 1)
    def _(place):
        who = flip(member, mixed_step(place, group), group)
        for kind in range(2):
            arrival(kind, who, landings(who)[kind]).wait_recv()

    @pl.loop(0, group)
    def _(who):
        key_land[who, :, HD:] = key_land[who, :, :HD]

    blocks = CHUNK // rows

    @pl.loop(0, group)
    def _(place):
        step = group - 1 - place
        who = flip(member, step, group)

        @pl.when(step > 0)
        def _():
            arrival(2, who, landings(who)[2]).wait_recv()

        scaled = query_land[who].astype(jnp.float32) * FACTOR
        high = scaled.astype(jnp.bfloat16)
        low = (scaled - high.astype(jnp.float32)).astype(jnp.bfloat16)
        pair = jnp.concatenate([high, low], axis=1)
        scores = lax.dot_general(pair, text_key[...], NT, preferred_element_type=jnp.float32)
        scores = scores + bias[...]
        top = jnp.max(scores, axis=1, keepdims=True)
        weights = jnp.exp2(scores - top).astype(jnp.bfloat16)
        total = jnp.dot(weights, text_value[...], preferred_element_type=jnp.float32)
        for first in range(0, group, blocks):
            keys = key_land[first : first + blocks].reshape(CHUNK, 2 * HD)
            values = value_land[first : first + blocks].reshape(CHUNK, 2 * HD)
            scores = lax.dot_general(pair, keys, NT, preferred_element_type=jnp.float32)
            new_top = jnp.maximum(top, jnp.max(scores, axis=1, keepdims=True))
            weights = jnp.exp2(scores - new_top).astype(jnp.bfloat16)
            total = total * jnp.exp2(top - new_top) + jnp.dot(
                weights, values, preferred_element_type=jnp.float32
            )
            top = new_top
        result[who] = (total[:, :HD] / total[:, HD:]).astype(jnp.bfloat16)

        @pl.when(step > 0)
        def _():
            remote(3, who, result.at[who], out_place(member)).start()

        @pl.when(step == 0)
        def _():
            pltpu.make_async_copy(result.at[who], out_place(member), own_sem.at[3]).start()

    pltpu.make_async_copy(result.at[member], out_place(member), own_sem.at[3]).wait()

    @pl.loop(1, group)
    def _(step):
        who = flip(member, group - step, group)
        arrival(3, who, out_place(who)).wait_recv()
        places = sources(who)
        for kind in range(3):
            remote(kind, who, places[kind], landings(member)[kind]).wait_send()
        remote(3, who, result.at[who], out_place(member)).wait_send()
        state_copy(who, member).wait_send()

    @pl.loop(1, seq_count)
    def _(step):
        part_copy(flip(seq_index, seq_count - step, seq_count), seq_index).wait_send()

    for step in range(1, tp_count):
        other = flip(tp_index, step, tp_count)
        mine = terms.at[tp_index]
        transfer("tp", other, mine, mine, term_send.at[other], term_recv.at[tp_index]).wait_send()
        mine = states.at[tp_index]
        transfer("tp", other, mine, mine, side_send.at[other], side_recv.at[tp_index]).wait_send()


def local(
    llama_context,
    llama_residual,
    w_attn_out,
    w_caption,
    w_text_kv,
    prompt_length,
    image_query,
    image_key,
    image_value,
):
    sides, rows, width = image_query.shape
    heads = width // HD
    group = IMG // rows
    units = sides * heads
    seq_count = lax.axis_size("seq")
    tp_count = lax.axis_size("tp")
    seq_index = lax.axis_index("seq")
    assert group % units == 0 and CHUNK % rows == 0
    query_rows = rows * units // group
    text_rows = TXT // group
    all_rows, features = llama_residual.shape
    depth = w_caption.shape[1]
    pair_index = seq_index // group
    pair_count = prompt_length.shape[0]
    live_length = jnp.sum(
        jnp.where(jnp.arange(pair_count, dtype=jnp.int32) == pair_index, prompt_length, 0)
    )
    bias = jnp.where(jnp.arange(TXT, dtype=jnp.int32) < live_length, 0.0, -1e30)
    head = seq_index % group % units % heads
    w_head = lax.dynamic_slice_in_dim(w_text_kv, head * HD, HD, axis=2)
    kinds = 4
    whole = pl.BlockSpec(memory_space=pl.ANY)
    vmem = pl.BlockSpec(memory_space=pltpu.VMEM)
    return pl.pallas_call(
        functools.partial(attend_kernel, group, sides, heads, seq_count, tp_count),
        out_shape=jax.ShapeDtypeStruct(image_query.shape, jnp.bfloat16),
        in_specs=[whole] * 3 + [vmem] * 6,
        out_specs=whole,
        scratch_shapes=[
            pltpu.VMEM((group, rows, 2 * HD), jnp.bfloat16),
            pltpu.VMEM((group, rows, 2 * HD), jnp.bfloat16),
            pltpu.VMEM((group, query_rows, HD), jnp.bfloat16),
            pltpu.VMEM((tp_count, all_rows, features), jnp.bfloat16),
            pltpu.VMEM((seq_count, text_rows, depth), jnp.bfloat16),
            pltpu.VMEM((seq_count, text_rows, depth), jnp.bfloat16),
            pltpu.VMEM((tp_count, group, text_rows, depth), jnp.bfloat16),
            pltpu.VMEM((TXT, 2 * HD), jnp.bfloat16),
            pltpu.VMEM((TXT, 2 * HD), jnp.bfloat16),
            pltpu.VMEM((group, query_rows, HD), jnp.bfloat16),
            pltpu.SemaphoreType.DMA((kinds,)),
            pltpu.SemaphoreType.DMA((kinds, group)),
            pltpu.SemaphoreType.DMA((kinds, group)),
            pltpu.SemaphoreType.DMA((tp_count,)),
            pltpu.SemaphoreType.DMA((tp_count,)),
            pltpu.SemaphoreType.DMA((seq_count,)),
            pltpu.SemaphoreType.DMA((seq_count,)),
            pltpu.SemaphoreType.DMA((group,)),
            pltpu.SemaphoreType.DMA((group,)),
            pltpu.SemaphoreType.DMA((tp_count,)),
            pltpu.SemaphoreType.DMA((tp_count,)),
        ],
        compiler_params=pltpu.CompilerParams(
            collective_id=0, has_side_effects=True, vmem_limit_bytes=48 * 2**20
        ),
        cost_estimate=pl.CostEstimate(
            flops=8 * image_query.size * (IMG + TXT),
            bytes_accessed=8 * image_query.size,
            transcendentals=group * query_rows * (IMG + TXT),
        ),
    )(
        image_query,
        image_key,
        image_value,
        llama_context,
        llama_residual,
        w_attn_out,
        w_caption,
        w_head.reshape(w_head.shape[0], 2 * HD),
        bias.astype(jnp.float32)[None, :],
    )


def solution(mesh):
    placed = (
        P(None, "tp"),
        P(None, "seq"),
        P("tp", "seq"),
        P("seq", "tp"),
        P(None, None, "tp"),
        P(),
        P(None, "seq", "tp"),
        P(None, "seq", "tp"),
        P(None, "seq", "tp"),
    )
    return jax.shard_map(
        local, mesh=mesh, in_specs=placed, out_specs=P(None, "seq", "tp"), check_vma=False
    )
```

profile of v0, /device:TPU:0, one launch (start us, length us, event | category | flops | bytes accessed | tf_op | source)
XLA Modules:
  0.0 125.3 jit_solution(12922934754947212843)
XLA Ops:
  0.7 0.0 copy-start.2
  0.7 0.0 copy-start.3
  0.7 0.0 copy-start.5
  0.7 2.8 %constant_dynamic-slice_fusion = bf16[2560,2,128]{2,1,0:T(2,128)(2,1)S(1)} fusion(bf16[2560,2,1024]{2,1,0:T(2,128)(2,1)} %param.13, s32[]{:T(128)S(6)} %select_n.40), kind=kLoop, calls=%fused_computation.2 | loop fusion | bytes 2621444 | tf_op jit(solution)/shard_map/dynamic_slice | solution.py:373
  3.5 0.0 copy-start
  3.5 0.0 copy-start.1
  3.5 0.0 copy-start.4
  3.5 1.2 copy.12
  4.8 0.0 copy-done.2
  4.8 0.0 copy-done.3
  4.8 0.0 copy-done.5
  4.8 0.2 copy-done
  5.0 0.6 copy-done.1
  5.5 0.1 copy-done.4
  5.6 118.7 %shard_map.91 = bf16[2,256,1024]{2,1,0:T(8,128)(2,1)S(1)} custom-call(bf16[2,256,1024]{2,1,0:T(8,128)(2,1)S(1)} %copy-done, bf16[2,256,1024]{2,1,0:T(8,128)(2,1)S(1)} %copy-done.1, bf16[2,256,1024]{2,1,0:T(8,128)(2,1)S(1)} %copy-done.2, bf16[128,2048]{1,0:T(8,128)(2,1)S(1)} %copy-done.4, bf16[128,256]{1,0:T(8,128)(2,1)S(1)} %copy-done.5, ...), custom_call_target="tpu_custom_call" | custom-call | flops 17716740096 | bytes 4194304 | tf_op jit(solution)/shard_map/pallas_call | solution.py:377
  124.3 1.0 copy.15
  (1 shorter events, 0.0 us)
Async XLA Ops:
  0.7 4.1 %copy-start.2 = (bf16[2,256,1024]{2,1,0:T(8,128)(2,1)S(1)}, bf16[2,256,1024]{2,1,0:T(8,128)(2,1)}, u32[]{:S(2)}) copy-start(bf16[2,256,1024]{2,1,0:T(8,128)(2,1)} %value.1) | copy-start | bytes 3145732
  0.7 4.1 %copy-start.3 = (bf16[256,1280]{1,0:T(8,128)(2,1)S(1)}, bf16[256,1280]{1,0:T(8,128)(2,1)}, u32[]{:S(2)}) copy-start(bf16[256,1280]{1,0:T(8,128)(2,1)} %w_caption.1) | copy-start | bytes 1966084
  0.7 4.1 %copy-start.5 = (bf16[128,256]{1,0:T(8,128)(2,1)S(1)}, bf16[128,256]{1,0:T(8,128)(2,1)}, u32[]{:S(2)}) copy-start(bf16[128,256]{1,0:T(8,128)(2,1)} %residual.1) | copy-start | bytes 196612
  3.5 1.5 %copy-start = (bf16[2,256,1024]{2,1,0:T(8,128)(2,1)S(1)}, bf16[2,256,1024]{2,1,0:T(8,128)(2,1)}, u32[]{:S(2)}) copy-start(bf16[2,256,1024]{2,1,0:T(8,128)(2,1)} %query.1) | copy-start | bytes 3145732
  3.5 2.0 %copy-start.1 = (bf16[2,256,1024]{2,1,0:T(8,128)(2,1)S(1)}, bf16[2,256,1024]{2,1,0:T(8,128)(2,1)}, u32[]{:S(2)}) copy-start(bf16[2,256,1024]{2,1,0:T(8,128)(2,1)} %key.1) | copy-start | bytes 3145732
  3.5 2.1 %copy-start.4 = (bf16[128,2048]{1,0:T(8,128)(2,1)S(1)}, bf16[128,2048]{1,0:T(8,128)(2,1)}, u32[]{:S(2)}) copy-start(bf16[128,2048]{1,0:T(8,128)(2,1)} %context.1) | copy-start | bytes 1572868
where the time goes:
time: 126 us; the launch traced here: 125 us
  Pallas kernels  119 us (94%)
  local copies, waits for them, and re-layouts  5.9 us (5%)
    pallas_call x1, Pallas kernels, local(): pl.pallas_call(functools.partial(attend_kernel, group, sides, heads, seq_...  119 us
    unnamed x14, local copies, waits for them, and re-layouts  3.11 us
    dynamic_slice x1, local copies, waits for them, and re-layouts, local(): w_head = lax.dynamic_slice_in_dim(w_text_kv, head * HD, HD, axis=2)  2.79 us

commit v1 on v0

--- a/solution.py
+++ b/solution.py
@@ -39,23 +39,32 @@
     query,
     key,
     value,
+    context_far,
+    residual_far,
+    w_out_far,
+    w_caption_far,
+    w_text_far,
+    bias,
+    out,
     context,
     residual,
     w_out,
     w_caption,
     w_head,
-    bias,
-    out,
     key_land,
     value_land,
     query_land,
     terms,
     parts,
+    chip_land,
+    chip_parts,
     parts_land,
     states,
     text_key,
     text_value,
     result,
+    load_sem,
+    core_sem,
     own_sem,
     send_sem,
     recv_sem,
@@ -83,6 +92,26 @@
     def columns(head):
         return pl.ds(pl.multiple_of(head * HD, HD), HD)
 
+    core = seq_index % 2
+    twin = flip(seq_index, 1, seq_count)
+    chip = seq_index // 2
+    chips = seq_count // 2
+    head_here = unit_of(member)[1]
+    loads = [
+        pltpu.make_async_copy(source, target, load_sem.at[index])
+        for index, (source, target) in enumerate(
+            (
+                (context_far, context),
+                (w_out_far, w_out),
+                (residual_far, residual),
+                (w_caption_far, w_caption),
+                (w_text_far.at[:, :, columns(head_here)], w_head),
+            )
+        )
+    ]
+    for load in loads:
+        load.start()
+
     barrier = pltpu.get_barrier_semaphore()
 
     @pl.loop(1, seq_count)
@@ -174,6 +203,8 @@
     for copy in own:
         copy.start()
 
+    loads[0].wait()
+    loads[1].wait()
     term = jnp.dot(context[...], w_out[...], preferred_element_type=jnp.float32)
     terms[tp_index] = term.astype(jnp.bfloat16)
     for step in range(1, tp_count):
@@ -190,51 +221,74 @@
     attended = terms[0].astype(jnp.float32)
     for index in range(1, tp_count):
         attended = attended + terms[index].astype(jnp.float32)
+    loads[2].wait()
+    loads[3].wait()
     hidden = (residual[...].astype(jnp.float32) + attended).astype(jnp.bfloat16)
     caption = jnp.dot(hidden, w_caption[...], preferred_element_type=jnp.float32)
-    parts[...] = caption.reshape(parts.shape).astype(jnp.bfloat16)
+    split = caption.reshape(chips, 2, parts.shape[2], parts.shape[3]).astype(jnp.bfloat16)
+    parts[0] = split[:, 0]
+    parts[1] = split[:, 1]
+    across = transfer(
+        "seq", twin, parts.at[1 - core], chip_land, core_sem.at[0], core_sem.at[1]
+    )
+    across.start()
+    wave(1, 0, half // 2)
+    across.wait_recv()
+    chip_parts[...] = (
+        parts[core].astype(jnp.float32) + chip_land[...].astype(jnp.float32)
+    ).astype(jnp.bfloat16)
 
     def part_copy(who, landed):
         return transfer(
             "seq",
-            who,
-            parts.at[who],
+            who * 2 + core,
+            chip_parts.at[who],
             parts_land.at[landed],
             part_send.at[who],
             part_recv.at[landed],
         )
 
-    @pl.loop(1, seq_count)
-    def _(step):
-        part_copy(flip(seq_index, seq_count - step, seq_count), seq_index).start()
-
-    parts_land[seq_index] = parts[seq_index]
-    wave(1, 0, half)
-
-    @pl.loop(1, seq_count)
-    def _(step):
-        who = flip(seq_index, seq_count - step, seq_count)
+    @pl.loop(1, chips)
+    def _(step):
+        part_copy(flip(chip, chips - step, chips), chip).start()
+
+    parts_land[chip] = chip_parts[chip]
+    wave(1, half // 2, half)
+
+    @pl.loop(1, chips)
+    def _(step):
+        who = flip(chip, chips - step, chips)
         part_copy(who, who).wait_recv()
 
     summed = jnp.sum(parts_land[...].astype(jnp.float32), axis=0)
-    states[tp_index, member] = summed.astype(jnp.bfloat16)
+    place = member // 2
+    places_here = group // 2
+    states[tp_index, core, place] = summed.astype(jnp.bfloat16)
 
     def state_copy(who, owner):
-        place = states.at[tp_index, owner]
+        block = states.at[tp_index, core, owner]
         return transfer(
-            "seq", base + who, place, place, state_send.at[who], state_recv.at[owner]
-        )
-
-    @pl.loop(1, group)
-    def _(step):
-        state_copy(flip(member, group - step, group), member).start()
-
-    wave(1, half, group - 1)
-
-    @pl.loop(1, group)
-    def _(step):
-        who = flip(member, group - step, group)
+            "seq", base + who * 2 + core, block, block, state_send.at[who], state_recv.at[owner]
+        )
+
+    @pl.loop(1, places_here)
+    def _(step):
+        state_copy(flip(place, places_here - step, places_here), place).start()
+
+    wave(1, half, half + half // 2)
+
+    @pl.loop(1, places_here)
+    def _(step):
+        who = flip(place, places_here - step, places_here)
         state_copy(who, who).wait_recv()
+
+    def states_across(half_from):
+        block = states.at[tp_index, half_from]
+        return transfer("seq", twin, block, block, core_sem.at[2], core_sem.at[3])
+
+    states_across(core).start()
+    wave(1, half + half // 2, group - 1)
+    states_across(1 - core).wait_recv()
 
     for step in range(1, tp_count):
         other = flip(tp_index, step, tp_count)
@@ -250,18 +304,19 @@
         theirs = states.at[other]
         transfer("tp", other, theirs, theirs, side_send.at[other], side_recv.at[other]).wait_recv()
     depth = w_caption.shape[1]
-    text = jnp.zeros((TXT, 2 * HD), jnp.float32)
+    loads[4].wait()
+    text = [jnp.zeros((TXT, HD), jnp.float32) for _ in range(2)]
     for index in range(tp_count):
         block = states[index].astype(jnp.float32).reshape(TXT, depth).astype(jnp.bfloat16)
-        text = text + jnp.dot(
-            block,
-            w_head[index * depth : (index + 1) * depth],
-            preferred_element_type=jnp.float32,
-        )
-    text = text.astype(jnp.bfloat16)
-    text_key[:, :HD] = text[:, :HD]
-    text_key[:, HD:] = text[:, :HD]
-    text_value[:, :HD] = text[:, HD:]
+        cut = pl.ds(index * depth, depth)
+        for kind in range(2):
+            text[kind] = text[kind] + jnp.dot(
+                block, w_head[cut, kind, :], preferred_element_type=jnp.float32
+            )
+    text_keys = text[0].astype(jnp.bfloat16)
+    text_key[:, :HD] = text_keys
+    text_key[:, HD:] = text_keys
+    text_value[:, :HD] = text[1].astype(jnp.bfloat16)
 
     for copy in own:
         copy.wait()
@@ -326,11 +381,17 @@
         for kind in range(3):
             remote(kind, who, places[kind], landings(member)[kind]).wait_send()
         remote(3, who, result.at[who], out_place(member)).wait_send()
-        state_copy(who, member).wait_send()
-
-    @pl.loop(1, seq_count)
-    def _(step):
-        part_copy(flip(seq_index, seq_count - step, seq_count), seq_index).wait_send()
+
+    @pl.loop(1, places_here)
+    def _(step):
+        state_copy(flip(place, places_here - step, places_here), place).wait_send()
+
+    @pl.loop(1, chips)
+    def _(step):
+        part_copy(flip(chip, chips - step, chips), chip).wait_send()
+
+    across.wait_send()
+    states_across(core).wait_send()
 
     for step in range(1, tp_count):
         other = flip(tp_index, step, tp_count)
@@ -361,6 +422,7 @@
     assert group % units == 0 and CHUNK % rows == 0
     query_rows = rows * units // group
     text_rows = TXT // group
+    chips = seq_count // 2
     all_rows, features = llama_residual.shape
     depth = w_caption.shape[1]
     pair_index = seq_index // group
@@ -368,37 +430,46 @@
     live_length = jnp.sum(
         jnp.where(jnp.arange(pair_count, dtype=jnp.int32) == pair_index, prompt_length, 0)
     )
-    bias = jnp.where(jnp.arange(TXT, dtype=jnp.int32) < live_length, 0.0, -1e30)
-    head = seq_index % group % units % heads
-    w_head = lax.dynamic_slice_in_dim(w_text_kv, head * HD, HD, axis=2)
+    tokens = jnp.arange(TXT, dtype=jnp.int32).reshape(group // 2, 2, text_rows)
+    tokens = tokens.transpose(1, 0, 2).reshape(TXT)
+    bias = jnp.where(tokens < live_length, 0.0, -1e30)
     kinds = 4
     whole = pl.BlockSpec(memory_space=pl.ANY)
     vmem = pl.BlockSpec(memory_space=pltpu.VMEM)
     return pl.pallas_call(
         functools.partial(attend_kernel, group, sides, heads, seq_count, tp_count),
         out_shape=jax.ShapeDtypeStruct(image_query.shape, jnp.bfloat16),
-        in_specs=[whole] * 3 + [vmem] * 6,
+        in_specs=[whole] * 8 + [vmem],
         out_specs=whole,
         scratch_shapes=[
+            pltpu.VMEM(llama_context.shape, jnp.bfloat16),
+            pltpu.VMEM(llama_residual.shape, jnp.bfloat16),
+            pltpu.VMEM(w_attn_out.shape, jnp.bfloat16),
+            pltpu.VMEM(w_caption.shape, jnp.bfloat16),
+            pltpu.VMEM(w_text_kv.shape[:2] + (HD,), jnp.bfloat16),
             pltpu.VMEM((group, rows, 2 * HD), jnp.bfloat16),
             pltpu.VMEM((group, rows, 2 * HD), jnp.bfloat16),
             pltpu.VMEM((group, query_rows, HD), jnp.bfloat16),
             pltpu.VMEM((tp_count, all_rows, features), jnp.bfloat16),
-            pltpu.VMEM((seq_count, text_rows, depth), jnp.bfloat16),
-            pltpu.VMEM((seq_count, text_rows, depth), jnp.bfloat16),
-            pltpu.VMEM((tp_count, group, text_rows, depth), jnp.bfloat16),
+            pltpu.VMEM((2, chips, text_rows, depth), jnp.bfloat16),
+            pltpu.VMEM((chips, text_rows, depth), jnp.bfloat16),
+            pltpu.VMEM((chips, text_rows, depth), jnp.bfloat16),
+            pltpu.VMEM((chips, text_rows, depth), jnp.bfloat16),
+            pltpu.VMEM((tp_count, 2, group // 2, text_rows, depth), jnp.bfloat16),
             pltpu.VMEM((TXT, 2 * HD), jnp.bfloat16),
             pltpu.VMEM((TXT, 2 * HD), jnp.bfloat16),
             pltpu.VMEM((group, query_rows, HD), jnp.bfloat16),
+            pltpu.SemaphoreType.DMA((5,)),
+            pltpu.SemaphoreType.DMA((4,)),
             pltpu.SemaphoreType.DMA((kinds,)),
             pltpu.SemaphoreType.DMA((kinds, group)),
             pltpu.SemaphoreType.DMA((kinds, group)),
             pltpu.SemaphoreType.DMA((tp_count,)),
             pltpu.SemaphoreType.DMA((tp_count,)),
-            pltpu.SemaphoreType.DMA((seq_count,)),
-            pltpu.SemaphoreType.DMA((seq_count,)),
-            pltpu.SemaphoreType.DMA((group,)),
-            pltpu.SemaphoreType.DMA((group,)),
+            pltpu.SemaphoreType.DMA((chips,)),
+            pltpu.SemaphoreType.DMA((chips,)),
+            pltpu.SemaphoreType.DMA((group // 2,)),
+            pltpu.SemaphoreType.DMA((group // 2,)),
             pltpu.SemaphoreType.DMA((tp_count,)),
             pltpu.SemaphoreType.DMA((tp_count,)),
         ],
@@ -418,7 +489,7 @@
         llama_residual,
         w_attn_out,
         w_caption,
-        w_head.reshape(w_head.shape[0], 2 * HD),
+        w_text_kv,
         bias.astype(jnp.float32)[None, :],
     )
 

time: 126 us -> 119 us (0.944)
  Pallas kernels: 119 us -> 110 us
  local copies, waits for them, and re-layouts: 5.9 us -> 7.69 us
    pallas_call x1, Pallas kernels: 119 us -> 110 us  [local(): pl.pallas_call(functools.partial(attend_kernel, group, sides, heads, seq_...]
    unnamed x14 -> x13, local copies, waits for them, and re-layouts: 3.11 us -> 7.61 us
    dynamic_slice x1 -> x0, local copies, waits for them, and re-layouts: 2.79 us -> none  [local(): w_head = lax.dynamic_slice_in_dim(w_text_kv, head * HD, HD, axis=2)]
where the time goes in v1:
time: 119 us
  Pallas kernels  110 us (92%)
  local copies, waits for them, and re-layouts  7.69 us (6%)
    pallas_call x1, Pallas kernels, local(): pl.pallas_call(functools.partial(attend_kernel, group, sides, heads, seq_...  110 us
    unnamed x13, local copies, waits for them, and re-layouts  7.61 us

profile of v1, /device:TPU:0, one launch (start us, length us, event | category | flops | bytes accessed | tf_op | source)
XLA Modules:
  0.0 118.8 jit_solution(1441433607667213838)
XLA Ops:
  0.7 0.1 reshape.75.bias
  0.8 0.0 copy-start
  0.8 1.2 %copy-done = bf16[2,256,1024]{2,1,0:T(8,128)(2,1)S(1)} copy-done((bf16[2,256,1024]{2,1,0:T(8,128)(2,1)S(1)}, bf16[2,256,1024]{2,1,0:T(8,128)(2,1)}, u32[]{:S(2)}) %copy-start) | copy-done | bytes 1048600
  2.0 0.0 copy-start.1
  2.0 1.2 %copy-done.1 = bf16[2,256,1024]{2,1,0:T(8,128)(2,1)S(1)} copy-done((bf16[2,256,1024]{2,1,0:T(8,128)(2,1)S(1)}, bf16[2,256,1024]{2,1,0:T(8,128)(2,1)}, u32[]{:S(2)}) %copy-start.1) | copy-done | bytes 1048600
  3.2 0.0 copy-start.2
  3.2 1.2 %copy-done.2 = bf16[2,256,1024]{2,1,0:T(8,128)(2,1)S(1)} copy-done((bf16[2,256,1024]{2,1,0:T(8,128)(2,1)S(1)}, bf16[2,256,1024]{2,1,0:T(8,128)(2,1)}, u32[]{:S(2)}) %copy-start.2) | copy-done | bytes 1048600
  4.4 0.0 copy-start.3
  4.4 1.1 copy-done.3
  5.5 0.0 copy-start.4
  5.5 1.0 copy-done.4
  6.6 0.0 copy-start.5
  6.6 0.8 copy-done.5
  7.4 110.5 %shard_map.91 = bf16[2,256,1024]{2,1,0:T(8,128)(2,1)S(1)} custom-call(bf16[2,256,1024]{2,1,0:T(8,128)(2,1)S(1)} %copy-done, bf16[2,256,1024]{2,1,0:T(8,128)(2,1)S(1)} %copy-done.1, bf16[2,256,1024]{2,1,0:T(8,128)(2,1)S(1)} %copy-done.2, bf16[128,2048]{1,0:T(8,128)(2,1)S(1)} %copy-done.4, bf16[128,256]{1,0:T(8,128)(2,1)S(1)} %copy-done.5, ...), custom_call_target="tpu_custom_call" | custom-call | flops 17716740096 | bytes 4194304 | tf_op jit(solution)/shard_map/pallas_call | solution.py:439
  117.9 1.0 copy.12
  (1 shorter events, 0.0 us)
Async XLA Ops:
  0.8 1.2 %copy-start = (bf16[2,256,1024]{2,1,0:T(8,128)(2,1)S(1)}, bf16[2,256,1024]{2,1,0:T(8,128)(2,1)}, u32[]{:S(2)}) copy-start(bf16[2,256,1024]{2,1,0:T(8,128)(2,1)} %query.1) | copy-start | bytes 3145732
  2.0 1.2 %copy-start.1 = (bf16[2,256,1024]{2,1,0:T(8,128)(2,1)S(1)}, bf16[2,256,1024]{2,1,0:T(8,128)(2,1)}, u32[]{:S(2)}) copy-start(bf16[2,256,1024]{2,1,0:T(8,128)(2,1)} %key.1) | copy-start | bytes 3145732
  3.2 1.2 %copy-start.2 = (bf16[2,256,1024]{2,1,0:T(8,128)(2,1)S(1)}, bf16[2,256,1024]{2,1,0:T(8,128)(2,1)}, u32[]{:S(2)}) copy-start(bf16[2,256,1024]{2,1,0:T(8,128)(2,1)} %value.1) | copy-start | bytes 3145732
  4.4 1.1 copy-start.3
  5.5 1.0 copy-start.4
  6.6 0.8 copy-start.5
